TPU v7x, 256 devices: a whole 4x4x8 slice. The times are simulated.
256 devices in a mesh: dp: 4 (over x), ep: 64 (over y, z, core).
Axes of the slice: x: 4, y: 4, z: 8, core: 2. Of those that a mesh axis runs over, the one named last changes fastest.
Arguments:
- tokens: bfloat16 [4, 2048, 2048], P('dp', 'ep'), may hold values from -12 to 12
- cotangent: bfloat16 [4, 2048, 2048], P('dp', 'ep'), may hold values from -6 to 6
- assign: int32 [4, 2048, 8], P('dp', 'ep'), may hold values from 0 to 63, as said below
- w_router: bfloat16 [2048, 64], replicated, may hold values from -0.125 to 0.125
- w_gate: bfloat16 [64, 2048, 768], P('ep'), may hold values from -0.125 to 0.125
- w_up: bfloat16 [64, 2048, 768], P('ep'), may hold values from -0.125 to 0.125
- w_down: bfloat16 [64, 2048, 768], P('ep'), may hold values from -0.21875 to 0.21875
Outputs:
- grad_tokens: bfloat16 [4, 2048, 2048], P('dp', 'ep')
- grad_router: float32 [2048, 64], replicated
- grad_gate: bfloat16 [64, 2048, 768], P('ep', 'dp')
- grad_up: bfloat16 [64, 2048, 768], P('ep', 'dp')
- grad_down: bfloat16 [64, 2048, 768], P('ep', 'dp')
Inputs may be any that keep to these rules, and one draw needn't show every extreme that they name: `assign`: each token names 8 different experts; the routes of the 32 tokens of one device name one expert at most 8 times, and in every draw one expert is named exactly 8 times by the routes of every device.
All inputs are finite; a program needn't handle non-finite values.
Results may differ from a plain program's by a relative error of at most 0.015.
Values may be sent and summed in bfloat16 or wider, within the bound.
A program may use at most 128 MiB of HBM per device.

v0:
```python
import jax
import jax.numpy as jnp
from jax import lax
from jax.sharding import PartitionSpec as P

ITERS = 3
cos_scale = 48.0
eps_norm = 1e-06
contract_first = (((0,), (0,)), ((), ()))
contract_last = (((1,), (1,)), ((), ()))


def logit_map(flat_tokens, router):
    inner_products = jnp.dot(flat_tokens, router, precision=lax.Precision.HIGHEST)
    token_norm = jnp.sqrt(jnp.sum(flat_tokens * flat_tokens, axis=1) + eps_norm)
    column_norm = jnp.sqrt(jnp.sum(router * router, axis=0) + eps_norm)
    return cos_scale * inner_products / (token_norm[:, None] * column_norm[None, :])


def expert_backward(expert_rows, expert_cotangent, rows_gate, gate_matrix, up_matrix, down_matrix):
    gate_linear = jnp.dot(expert_rows, gate_matrix, preferred_element_type=jnp.float32)
    up_linear = jnp.dot(expert_rows, up_matrix, preferred_element_type=jnp.float32)
    sigmoid_gate = jax.nn.sigmoid(gate_linear)
    activation = gate_linear * sigmoid_gate
    product = activation * up_linear
    hidden = product.astype(jnp.bfloat16)
    weighted = (rows_gate[:, None] * product).astype(jnp.bfloat16)
    raw_back = jnp.dot(expert_cotangent, down_matrix, preferred_element_type=jnp.float32)
    gate_grad = jnp.sum(raw_back * hidden.astype(jnp.float32), axis=1).astype(jnp.bfloat16)
    scaled_back = rows_gate[:, None] * raw_back
    up_delta = (scaled_back * activation).astype(jnp.bfloat16)
    gate_delta = (
        scaled_back * up_linear * sigmoid_gate * (1.0 + gate_linear * (1.0 - sigmoid_gate))
    ).astype(jnp.bfloat16)
    route_back = (
        lax.dot_general(gate_delta, gate_matrix, contract_last, preferred_element_type=jnp.float32)
        + lax.dot_general(up_delta, up_matrix, contract_last, preferred_element_type=jnp.float32)
    ).astype(jnp.bfloat16)
    return (gate_grad, route_back, gate_delta, up_delta, weighted)


def column_sums(values):
    return lax.psum(jnp.sum(values, axis=0), "ep")


def per_device(tokens, cotangent, assign, w_router, w_gate, w_up, w_down):
    local_tokens = tokens[0]
    local_cotangent = cotangent[0]
    route_ids = assign[0]
    token_count, per_token = route_ids.shape
    model_width = local_tokens.shape[1]
    experts = w_router.shape[1]
    slot_cap = min(token_count, 2 * token_count * per_token // experts)
    logits, logit_vjp = jax.vjp(
        logit_map, local_tokens.astype(jnp.float32), w_router.astype(jnp.float32)
    )
    kernel_start = jnp.exp(logits)
    kernel = kernel_start
    saved_steps = []
    for sweep_index in range(ITERS):
        column = column_sums(kernel)
        scaled = kernel / column[None, :]
        row_total = jnp.sum(scaled, axis=1, keepdims=True)
        kernel = scaled / row_total
        saved_steps.append((column, scaled, row_total, kernel))
    expert_ids = jnp.arange(experts, dtype=jnp.int32)
    onehot = (route_ids[:, :, None] == expert_ids).astype(jnp.float32)
    picked = jnp.sum(onehot * kernel[:, None, :], axis=2)
    picked_sum = jnp.sum(picked, axis=1, keepdims=True)
    gates = picked / picked_sum
    gate_half = gates.astype(jnp.bfloat16)
    flat_route = route_ids.reshape(-1)
    member = (flat_route[:, None] == expert_ids).astype(jnp.int32)
    earlier = jnp.cumsum(member, axis=0) - member
    slot_index = jnp.sum(earlier * member, axis=1)
    target = flat_route * slot_cap + slot_index
    route_slots = (
        jnp.arange(experts * slot_cap, dtype=jnp.int32)[:, None] == target[None, :]
    ).astype(jnp.bfloat16)
    token_slots = jnp.sum(route_slots.reshape(experts * slot_cap, token_count, per_token), axis=2)
    send_tokens = jnp.dot(token_slots, local_tokens, preferred_element_type=jnp.float32).astype(
        jnp.bfloat16
    )
    send_cotangent = jnp.dot(
        token_slots, local_cotangent, preferred_element_type=jnp.float32
    ).astype(jnp.bfloat16)
    send_gate = jnp.dot(
        route_slots, gate_half.reshape(-1), preferred_element_type=jnp.float32
    ).astype(jnp.bfloat16)
    recv_tokens, recv_cotangent, recv_gate = (
        lax.all_to_all(
            send_tokens.reshape(experts, slot_cap, model_width),
            "ep",
            split_axis=0,
            concat_axis=0,
            tiled=True,
        ),
        lax.all_to_all(
            send_cotangent.reshape(experts, slot_cap, model_width),
            "ep",
            split_axis=0,
            concat_axis=0,
            tiled=True,
        ),
        lax.all_to_all(
            send_gate.reshape(experts, slot_cap), "ep", split_axis=0, concat_axis=0, tiled=True
        ),
    )
    expert_rows = recv_tokens.reshape(-1, model_width)
    expert_cotangent = recv_cotangent.reshape(-1, model_width)
    rows_gate = recv_gate.reshape(-1).astype(jnp.float32)
    gate_grad, route_back, gate_delta, up_delta, weighted = expert_backward(
        expert_rows, expert_cotangent, rows_gate, w_gate[0], w_up[0], w_down[0]
    )
    back_rows, back_gate = (
        lax.all_to_all(
            route_back.reshape(experts, slot_cap, model_width),
            "ep",
            split_axis=0,
            concat_axis=0,
            tiled=True,
        ),
        lax.all_to_all(
            gate_grad.reshape(experts, slot_cap), "ep", split_axis=0, concat_axis=0, tiled=True
        ),
    )
    expert_back = lax.dot_general(
        token_slots,
        back_rows.reshape(-1, model_width),
        contract_first,
        preferred_element_type=jnp.float32,
    )
    route_grad = lax.dot_general(
        route_slots, back_gate.reshape(-1), contract_first, preferred_element_type=jnp.float32
    ).reshape(token_count, per_token)
    hidden_units = gate_delta.shape[1]
    summed = lax.psum_scatter(
        jnp.concatenate(
            [
                lax.dot_general(
                    expert_rows, gate_delta, contract_first, preferred_element_type=jnp.float32
                ),
                lax.dot_general(
                    expert_rows, up_delta, contract_first, preferred_element_type=jnp.float32
                ),
                lax.dot_general(
                    expert_cotangent, weighted, contract_first, preferred_element_type=jnp.float32
                ),
            ],
            axis=1,
        ).astype(jnp.bfloat16),
        "dp",
        scatter_dimension=0,
        tiled=True,
    ).astype(jnp.float32)
    grad_gate = summed[:, :hidden_units]
    grad_up = summed[:, hidden_units : 2 * hidden_units]
    grad_down = summed[:, 2 * hidden_units :]
    picked_grad = (route_grad - jnp.sum(route_grad * gates, axis=1, keepdims=True)) / picked_sum
    kernel_grad = jnp.sum(onehot * picked_grad[:, :, None], axis=1)
    for sweep_index in reversed(range(ITERS)):
        column, scaled, row_total, kernel_step = saved_steps[sweep_index]
        scaled_grad = (
            kernel_grad - jnp.sum(kernel_grad * kernel_step, axis=1, keepdims=True)
        ) / row_total
        moment = lax.psum(jnp.sum(scaled_grad * scaled, axis=0), "ep")
        kernel_grad = (scaled_grad - moment[None, :]) / column[None, :]
    logit_grad = kernel_grad * kernel_start
    router_back, router_part = logit_vjp(logit_grad)
    grad_router = lax.psum(router_part, ("dp", "ep"))
    grad_tokens = (expert_back + router_back).astype(jnp.bfloat16)[None]
    return (
        grad_tokens,
        grad_router,
        grad_gate.astype(jnp.bfloat16)[None],
        grad_up.astype(jnp.bfloat16)[None],
        grad_down.astype(jnp.bfloat16)[None],
    )


def solution(mesh):
    return jax.shard_map(
        per_device,
        mesh=mesh,
        in_specs=(
            P("dp", "ep", None),
            P("dp", "ep", None),
            P("dp", "ep", None),
            P(),
            P("ep", None, None),
            P("ep", None, None),
            P("ep", None, None),
        ),
        out_specs=(
            P("dp", "ep", None),
            P(),
            P("ep", "dp", None),
            P("ep", "dp", None),
            P("ep", "dp", None),
        ),
        check_vma=False,
    )
```

profile of v0, /device:TPU:2, one launch (start us, length us, event | category | flops | bytes accessed | tf_op | source)
XLA Modules:
  0.0 1251.3 jit_solution(17761611733418999477)
XLA Ops:
  15.1 131.8 %psum.49 = f32[64]{0:T(128)S(1)} all-reduce(f32[64]{0:T(128)S(1)} %get-tuple-element.33), channel_id=1, replica_groups=mesh['dp'=4,'ep'=64] {'ep'}, use_global_device_ids=true, to_apply=%region_7.0 | all-reduce | flops 64 | bytes 512 | tf_op jit(solution)/shard_map/psum | solution.py:43
  147.1 124.1 %psum.50 = f32[64]{0:T(128)S(1)} all-reduce(f32[64]{0:T(128)S(1)} %fusion.67), channel_id=1, replica_groups=mesh['dp'=4,'ep'=64] {'ep'}, use_global_device_ids=true, to_apply=%region_10.0 | all-reduce | flops 64 | bytes 512 | tf_op jit(solution)/shard_map/psum | solution.py:43
  271.4 124.0 %psum.51 = f32[64]{0:T(128)S(1)} all-reduce(f32[64]{0:T(128)S(1)} %fusion.73), channel_id=1, replica_groups=mesh['dp'=4,'ep'=64] {'ep'}, use_global_device_ids=true, to_apply=%region_13.0 | all-reduce | flops 64 | bytes 512 | tf_op jit(solution)/shard_map/psum | solution.py:43
  398.9 4.6 all-to-all-start
  403.9 2.9 fusion.13
  406.9 6.1 all-to-all-done
  413.0 5.6 all-to-all-start.2
  418.6 2.1 fusion.12
  420.6 49.0 %all-to-all-done.2 = bf16[64,8,2048]{2,1,0:T(8,128)(2,1)} async-done(((bf16[64,8,2048]{2,1,0:T(8,128)(2,1)}), bf16[64,8,2048]{2,1,0:T(8,128)(2,1)}, u32[]{:S(2)}, u32[]{:S(2)}) %all-to-all-start.2) | async-done | bytes 2097184 | tf_op jit(solution)/shard_map/all_to_all | solution.py:91
  469.6 6.1 all-to-all-start.1
  476.1 5.5 fusion.6
  481.6 4.6 fusion.2
  486.2 40.5 %all-to-all-done.1 = bf16[64,8,2048]{2,1,0:T(8,128)(2,1)} async-done(((bf16[64,8,2048]{2,1,0:T(8,128)(2,1)}), bf16[64,8,2048]{2,1,0:T(8,128)(2,1)}, u32[]{:S(2)}, u32[]{:S(2)}) %all-to-all-start.1) | async-done | bytes 2097184 | tf_op jit(solution)/shard_map/all_to_all | solution.py:98
  526.7 4.6 convolution_convert_fusion
  531.4 4.0 multiply_reduce_fusion
  535.4 4.0 convolution_convert_fusion.1
  539.5 3.4 convolution_convert_fusion.2
  542.9 4.5 pad_maximum_fusion
  548.1 6.4 all-to-all-start.4
  554.5 3.3 fusion
  557.8 3.1 fusion.14
  560.9 2.6 all-to-all-done.4
  563.5 7.7 all-to-all-start.3
  580.8 155.9 %psum.52 = f32[64]{0:T(128)} all-reduce(f32[64]{0:T(128)} %multiply_reduce_fusion.7), channel_id=1, replica_groups=mesh['dp'=4,'ep'=64] {'ep'}, use_global_device_ids=true, to_apply=%region_22.23 | all-reduce | flops 64 | bytes 512 | tf_op jit(solution)/shard_map/psum | solution.py:166
  739.6 124.5 %psum.53 = f32[64]{0:T(128)} all-reduce(f32[64]{0:T(128)} %get-tuple-element.31), channel_id=1, replica_groups=mesh['dp'=4,'ep'=64] {'ep'}, use_global_device_ids=true, to_apply=%region_25.26 | all-reduce | flops 64 | bytes 512 | tf_op jit(solution)/shard_map/psum | solution.py:166
  866.9 124.7 %psum.54 = f32[64]{0:T(128)} all-reduce(f32[64]{0:T(128)} %multiply_reduce_fusion.3), channel_id=1, replica_groups=mesh['dp'=4,'ep'=64] {'ep'}, use_global_device_ids=true, to_apply=%region_28.29 | all-reduce | flops 64 | bytes 512 | tf_op jit(solution)/shard_map/psum | solution.py:166
  997.6 2.1 fusion.21
  1000.8 3.1 slice_bitcast_fusion
  1003.8 2.3 copy.39
  1006.1 2.3 copy.40
  1008.4 2.3 copy.41
  1010.7 231.3 %all-reduce.2.cloned.1.call-done = f32[2048,64]{0,1:T(8,128)} async-done(((f32[2048,64]{0,1:T(8,128)}), f32[2048,64]{0,1:T(8,128)}) %all-reduce.2.cloned.1.call-update) | async-done | bytes 524304 | tf_op jit(solution)/shard_map/psum | solution.py:170
  (126 shorter events, 36.5 us)
Async XLA Ops:
  8.0 473.6 %copy-start = (bf16[1,2048,768]{2,1,0:T(8,128)(2,1)S(1)}, bf16[1,2048,768]{2,1,0:T(8,128)(2,1)}, u32[]{:S(2)}) copy-start(bf16[1,2048,768]{2,1,0:T(8,128)(2,1)} %param.11) | copy-start | bytes 9437188
  8.9 404.0 %copy-start.3 = (s32[1,32,8]{2,1,0:T(8,128)}, s32[1,32,8]{2,1,0:T(8,128)S(1)}, u32[]{:S(2)}) copy-start(s32[1,32,8]{2,1,0:T(8,128)S(1)} %copy.33) | copy-start | bytes 3076
  11.6 3.5 copy-start.16
  13.3 1.8 copy-start.18
  146.9 257.0 %copy-start.10 = (f32[64]{0:T(128)}, f32[64]{0:T(128)S(1)}, u32[]{:S(2)}) copy-start(f32[64]{0:T(128)S(1)} %psum.49) | copy-start | bytes 772
  147.0 256.9 %copy-start.11 = (f32[32]{0:T(128)}, f32[32]{0:T(128)S(1)}, u32[]{:S(2)}) copy-start(f32[32]{0:T(128)S(1)} %fusion.65) | copy-start | bytes 388
  271.2 132.7 %copy-start.12 = (f32[64]{0:T(128)}, f32[64]{0:T(128)S(1)}, u32[]{:S(2)}) copy-start(f32[64]{0:T(128)S(1)} %psum.50) | copy-start | bytes 772
  271.3 132.6 %copy-start.13 = (f32[32]{0:T(128)}, f32[32]{0:T(128)S(1)}, u32[]{:S(2)}) copy-start(f32[32]{0:T(128)S(1)} %fusion.70) | copy-start | bytes 388
  396.8 7.2 copy-start.21
  398.9 14.0 %all-to-all-start = ((bf16[64,1,8]{2,1,0:T(2,128)(2,1)}), bf16[64,1,8]{2,1,0:T(2,128)(2,1)S(1)}, u32[]{:S(2)}, u32[]{:S(2)}) async-start(bf16[64,1,8]{2,1,0:T(2,128)(2,1)} %all_to_all.25), calls=%async_computation | async-start | bytes 65536 | tf_op jit(solution)/shard_map/all_to_all | solution.py:105
  403.9 14.6 %copy-start.4 = (bf16[512,32]{0,1:T(8,128)(2,1)}, bf16[512,32]{0,1:T(8,128)(2,1)S(1)}, u32[]{:S(2)}) copy-start(bf16[512,32]{0,1:T(8,128)(2,1)S(1)} %fusion.41) | copy-start | bytes 98308
  406.9 11.7 copy-start.9
  413.0 56.6 %all-to-all-start.2 = ((bf16[64,8,2048]{2,1,0:T(8,128)(2,1)}), bf16[64,8,2048]{2,1,0:T(8,128)(2,1)}, u32[]{:S(2)}, u32[]{:S(2)}) async-start(bf16[64,8,2048]{2,1,0:T(8,128)(2,1)} %fusion.13), calls=%async_computation.2 | async-start | bytes 4194304 | tf_op jit(solution)/shard_map/all_to_all | solution.py:91
  469.6 57.2 %all-to-all-start.1 = ((bf16[64,8,2048]{2,1,0:T(8,128)(2,1)}), bf16[64,8,2048]{2,1,0:T(8,128)(2,1)}, u32[]{:S(2)}, u32[]{:S(2)}) async-start(bf16[64,8,2048]{2,1,0:T(8,128)(2,1)} %fusion.12), calls=%async_computation.1 | async-start | bytes 4194304 | tf_op jit(solution)/shard_map/all_to_all | solution.py:98
  475.7 525.0 %reduce-scatter.2.cloned.1.call-start = ((), (), s32[]{:S(2)}) async-start(), calls=%async_computation.7 | async-start | bytes 11796480 | tf_op jit(solution)/shard_map/reduce_scatter | solution.py:137
  526.7 4.6 copy-start.27
  526.7 4.7 copy-start.32
  526.7 4.7 copy-start.33
  535.4 4.0 copy-start.29
  535.4 4.0 copy-start.31
  548.1 15.4 %all-to-all-start.4 = ((bf16[64,1,8]{2,1,0:T(2,128)(2,1)}), bf16[64,1,8]{2,1,0:T(2,128)(2,1)}, u32[]{:S(2)}, u32[]{:S(2)}) async-start(bf16[64,1,8]{2,1,0:T(2,128)(2,1)} %convert_element_type.108), calls=%async_computation.4 | async-start | bytes 65536 | tf_op jit(solution)/shard_map/all_to_all | solution.py:123
  554.5 3.3 copy-start.28
  554.5 3.3 copy-start.30
  560.9 433.5 %copy-start.1 = (bf16[2048,64]{0,1:T(8,128)(2,1)S(1)}, bf16[2048,64]{0,1:T(8,128)(2,1)}, u32[]{:S(2)}) copy-start(bf16[2048,64]{0,1:T(8,128)(2,1)} %param.10) | copy-start | bytes 786436
  560.9 433.5 %copy-start.2 = (bf16[1,32,2048]{2,1,0:T(8,128)(2,1)S(1)}, bf16[1,32,2048]{2,1,0:T(8,128)(2,1)}, u32[]{:S(2)}) copy-start(bf16[1,32,2048]{2,1,0:T(8,128)(2,1)} %param.7) | copy-start | bytes 393220
  563.5 434.1 %all-to-all-start.3 = ((bf16[64,8,2048]{2,1,0:T(8,128)(2,1)}), bf16[64,8,2048]{2,1,0:T(8,128)(2,1)}, u32[]{:S(2)}, u32[]{:S(2)}) async-start(bf16[64,8,2048]{2,1,0:T(8,128)(2,1)} %fusion.14), calls=%async_computation.3 | async-start | bytes 4194304 | tf_op jit(solution)/shard_map/all_to_all | solution.py:116
  571.2 670.8 %all-reduce.2.cloned.1.call-start = ((), (), s32[]{:S(2)}) async-start(), calls=%async_computation.6 | async-start | bytes 1048576 | tf_op jit(solution)/shard_map/psum | solution.py:170
  992.5 2.0 copy-start.6
  996.4 3.3 copy-start.7
  997.6 2.1 copy-start.17
  997.6 2.1 copy-start.19
  997.6 2.1 copy-start.26
  (9 other events, 6.1 us)
Sparse Core Ops, SparseCore 0:
  547.5 87.0 reduce-scatter.1
Sparse Core Ops, SparseCore 1:
  996.5 245.4 all-reduce.1
where the time goes:
time: 1250 us
  blocking collectives  785 us (63%)
  waiting for transfers between devices  330 us (26%)
  matrix products  46 us (4%)
  starting transfers between devices  30.6 us (2%)
  other arithmetic  24.4 us (2%)
  local copies, waits for them, and re-layouts  19.8 us (2%)
  between operations  16 us (1%)
    psum x3, blocking collectives, per_device(): moment = lax.psum(jnp.sum(scaled_grad * scaled, axis=0), 'ep')  405 us
    psum x3, blocking collectives, column_sums(): return lax.psum(jnp.sum(values, axis=0), 'ep')  380 us
    psum x1, waiting for transfers between devices, per_device(): grad_router = lax.psum(router_part, ('dp', 'ep'))  231 us
    all_to_all x1, waiting for transfers between devices, per_device(): lax.all_to_all(send_tokens.reshape(experts, slot_cap, model_width), 'ep',...  49 us
    all_to_all x1, waiting for transfers between devices, per_device(): lax.all_to_all(send_cotangent.reshape(experts, slot_cap, model_width), 'e...  40.5 us
  transfers between devices with their start and end apart: 7, of which 5 were waited for; matrix products, arithmetic and copies ran while one was open for 4% of the time, Pallas kernels for 0%

commit v1 on v0

--- a/solution.py
+++ b/solution.py
@@ -163,7 +163,7 @@
         scaled_grad = (
             kernel_grad - jnp.sum(kernel_grad * kernel_step, axis=1, keepdims=True)
         ) / row_total
-        moment = lax.psum(jnp.sum(scaled_grad * scaled, axis=0), "ep")
+        moment = jnp.sum(lax.all_gather(jnp.sum(scaled_grad * scaled, axis=0), "ep"), axis=0)
         kernel_grad = (scaled_grad - moment[None, :]) / column[None, :]
     logit_grad = kernel_grad * kernel_start
     router_back, router_part = logit_vjp(logit_grad)

time: 1250 us -> 1630 us (1.30)
  blocking collectives: 785 us -> 1150 us
    unnamed x0 -> x3, blocking collectives: none -> 766 us
    psum x3 -> x0, blocking collectives: 405 us -> none  [per_device(): moment = lax.psum(jnp.sum(scaled_grad * scaled, axis=0), 'ep')]
where the time goes in v1:
time: 1630 us
  blocking collectives  1150 us (71%)
  waiting for transfers between devices  330 us (20%)
  matrix products  46 us (3%)
  local copies, waits for them, and re-layouts  31 us (2%)
  starting transfers between devices  30.6 us (2%)
  other arithmetic  28.3 us (2%)
  between operations  16.6 us (1%)
    unnamed x3, blocking collectives  766 us
    psum x3, blocking collectives, column_sums(): return lax.psum(jnp.sum(values, axis=0), 'ep')  380 us
    psum x1, waiting for transfers between devices, per_device(): grad_router = lax.psum(router_part, ('dp', 'ep'))  231 us
    all_to_all x1, waiting for transfers between devices, per_device(): lax.all_to_all(send_tokens.reshape(experts, slot_cap, model_width), 'ep',...  49 us
    all_to_all x1, waiting for transfers between devices, per_device(): lax.all_to_all(send_cotangent.reshape(experts, slot_cap, model_width), 'e...  40.5 us
  transfers between devices with their start and end apart: 7, of which 5 were waited for; matrix products, arithmetic and copies ran while one was open for 4% of the time, Pallas kernels for 0%

profile of v1, /device:TPU:2, one launch (start us, length us, event | category | flops | bytes accessed | tf_op | source)
XLA Modules:
  0.0 1628.1 jit_solution(1117943553563010411)
XLA Ops:
  15.1 131.8 %psum.28 = f32[64]{0:T(128)S(1)} all-reduce(f32[64]{0:T(128)S(1)} %get-tuple-element.33), channel_id=1, replica_groups=mesh['dp'=4,'ep'=64] {'ep'}, use_global_device_ids=true, to_apply=%region_7.0 | all-reduce | flops 64 | bytes 512 | tf_op jit(solution)/shard_map/psum | solution.py:43
  147.1 124.1 %psum.29 = f32[64]{0:T(128)S(1)} all-reduce(f32[64]{0:T(128)S(1)} %fusion.67), channel_id=1, replica_groups=mesh['dp'=4,'ep'=64] {'ep'}, use_global_device_ids=true, to_apply=%region_10.0 | all-reduce | flops 64 | bytes 512 | tf_op jit(solution)/shard_map/psum | solution.py:43
  271.4 124.0 %psum.30 = f32[64]{0:T(128)S(1)} all-reduce(f32[64]{0:T(128)S(1)} %fusion.73), channel_id=1, replica_groups=mesh['dp'=4,'ep'=64] {'ep'}, use_global_device_ids=true, to_apply=%region_13.0 | all-reduce | flops 64 | bytes 512 | tf_op jit(solution)/shard_map/psum | solution.py:43
  398.9 4.6 all-to-all-start
  403.9 2.9 fusion.13
  406.9 6.1 all-to-all-done
  413.0 5.6 all-to-all-start.2
  418.6 2.1 fusion.12
  420.6 49.0 %all-to-all-done.2 = bf16[64,8,2048]{2,1,0:T(8,128)(2,1)} async-done(((bf16[64,8,2048]{2,1,0:T(8,128)(2,1)}), bf16[64,8,2048]{2,1,0:T(8,128)(2,1)}, u32[]{:S(2)}, u32[]{:S(2)}) %all-to-all-start.2) | async-done | bytes 2097184 | tf_op jit(solution)/shard_map/all_to_all | solution.py:91
  469.6 6.1 all-to-all-start.1
  476.1 5.5 fusion.6
  481.6 4.6 fusion.2
  486.2 40.5 %all-to-all-done.1 = bf16[64,8,2048]{2,1,0:T(8,128)(2,1)} async-done(((bf16[64,8,2048]{2,1,0:T(8,128)(2,1)}), bf16[64,8,2048]{2,1,0:T(8,128)(2,1)}, u32[]{:S(2)}, u32[]{:S(2)}) %all-to-all-start.1) | async-done | bytes 2097184 | tf_op jit(solution)/shard_map/all_to_all | solution.py:98
  526.7 4.6 convolution_convert_fusion
  531.4 4.0 multiply_reduce_fusion
  535.4 4.0 convolution_convert_fusion.1
  539.5 3.4 convolution_convert_fusion.2
  542.9 4.5 pad_maximum_fusion
  548.1 6.4 all-to-all-start.4
  554.5 3.3 fusion
  557.8 3.1 fusion.14
  560.9 2.6 all-to-all-done.4
  563.5 7.7 all-to-all-start.3
  584.3 273.9 %all-reduce = f32[4096]{0:T(1024)} all-reduce(f32[4096]{0:T(1024)} %dynamic-update-slice), channel_id=2, replica_groups=mesh['dp'=4,'ep'=64] {'ep'}, use_global_device_ids=true, to_apply=%add | all-reduce | flops 4096 | bytes 32768
  865.8 246.1 %all-reduce.1 = f32[4096]{0:T(1024)} all-reduce(f32[4096]{0:T(1024)} %dynamic-update-slice.1), channel_id=3, replica_groups=mesh['dp'=4,'ep'=64] {'ep'}, use_global_device_ids=true, to_apply=%add.1 | all-reduce | flops 4096 | bytes 32768
  1119.5 246.1 %all-reduce.2 = f32[4096]{0:T(1024)} all-reduce(f32[4096]{0:T(1024)} %dynamic-update-slice.2), channel_id=4, replica_groups=mesh['dp'=4,'ep'=64] {'ep'}, use_global_device_ids=true, to_apply=%add.2 | all-reduce | flops 4096 | bytes 32768
  1374.4 2.1 fusion.21
  1377.5 3.1 slice_bitcast_fusion
  1380.6 2.3 copy.39
  1382.9 2.3 copy.40
  1385.2 2.3 copy.41
  1387.5 231.3 %all-reduce.5.cloned.1.call-done = f32[2048,64]{0,1:T(8,128)} async-done(((f32[2048,64]{0,1:T(8,128)}), f32[2048,64]{0,1:T(8,128)}) %all-reduce.5.cloned.1.call-update) | async-done | bytes 524304 | tf_op jit(solution)/shard_map/psum | solution.py:170
  (139 shorter events, 51.6 us)
Async XLA Ops:
  8.0 473.6 %copy-start = (bf16[1,2048,768]{2,1,0:T(8,128)(2,1)S(1)}, bf16[1,2048,768]{2,1,0:T(8,128)(2,1)}, u32[]{:S(2)}) copy-start(bf16[1,2048,768]{2,1,0:T(8,128)(2,1)} %param.11) | copy-start | bytes 9437188
  8.9 404.0 %copy-start.3 = (s32[1,32,8]{2,1,0:T(8,128)}, s32[1,32,8]{2,1,0:T(8,128)S(1)}, u32[]{:S(2)}) copy-start(s32[1,32,8]{2,1,0:T(8,128)S(1)} %copy.33) | copy-start | bytes 3076
  11.6 3.5 copy-start.16
  13.3 1.8 copy-start.18
  146.9 257.0 %copy-start.10 = (f32[64]{0:T(128)}, f32[64]{0:T(128)S(1)}, u32[]{:S(2)}) copy-start(f32[64]{0:T(128)S(1)} %psum.28) | copy-start | bytes 772
  147.0 256.9 %copy-start.11 = (f32[32]{0:T(128)}, f32[32]{0:T(128)S(1)}, u32[]{:S(2)}) copy-start(f32[32]{0:T(128)S(1)} %fusion.65) | copy-start | bytes 388
  271.2 132.7 %copy-start.12 = (f32[64]{0:T(128)}, f32[64]{0:T(128)S(1)}, u32[]{:S(2)}) copy-start(f32[64]{0:T(128)S(1)} %psum.29) | copy-start | bytes 772
  271.3 132.6 %copy-start.13 = (f32[32]{0:T(128)}, f32[32]{0:T(128)S(1)}, u32[]{:S(2)}) copy-start(f32[32]{0:T(128)S(1)} %fusion.70) | copy-start | bytes 388
  396.8 7.2 copy-start.21
  398.9 14.0 all-to-all-start
  403.9 14.6 copy-start.4
  406.9 11.7 copy-start.9
  413.0 56.6 %all-to-all-start.2 = ((bf16[64,8,2048]{2,1,0:T(8,128)(2,1)}), bf16[64,8,2048]{2,1,0:T(8,128)(2,1)}, u32[]{:S(2)}, u32[]{:S(2)}) async-start(bf16[64,8,2048]{2,1,0:T(8,128)(2,1)} %fusion.13), calls=%async_computation.2 | async-start | bytes 4194304 | tf_op jit(solution)/shard_map/all_to_all | solution.py:91
  469.6 57.2 %all-to-all-start.1 = ((bf16[64,8,2048]{2,1,0:T(8,128)(2,1)}), bf16[64,8,2048]{2,1,0:T(8,128)(2,1)}, u32[]{:S(2)}, u32[]{:S(2)}) async-start(bf16[64,8,2048]{2,1,0:T(8,128)(2,1)} %fusion.12), calls=%async_computation.1 | async-start | bytes 4194304 | tf_op jit(solution)/shard_map/all_to_all | solution.py:98
  475.7 901.8 %reduce-scatter.2.cloned.1.call-start = ((), (), s32[]{:S(2)}) async-start(), calls=%async_computation.7 | async-start | bytes 11796480 | tf_op jit(solution)/shard_map/reduce_scatter | solution.py:137
  526.7 4.6 copy-start.27
  526.7 4.7 copy-start.32
  526.7 4.7 copy-start.33
  535.4 4.0 copy-start.29
  535.4 4.0 copy-start.31
  548.1 15.4 all-to-all-start.4
  554.5 3.3 copy-start.28
  554.5 3.3 copy-start.30
  560.9 810.3 %copy-start.1 = (bf16[2048,64]{0,1:T(8,128)(2,1)S(1)}, bf16[2048,64]{0,1:T(8,128)(2,1)}, u32[]{:S(2)}) copy-start(bf16[2048,64]{0,1:T(8,128)(2,1)} %param.10) | copy-start | bytes 786436
  560.9 810.3 %copy-start.2 = (bf16[1,32,2048]{2,1,0:T(8,128)(2,1)S(1)}, bf16[1,32,2048]{2,1,0:T(8,128)(2,1)}, u32[]{:S(2)}) copy-start(bf16[1,32,2048]{2,1,0:T(8,128)(2,1)} %param.7) | copy-start | bytes 393220
  563.5 810.8 %all-to-all-start.3 = ((bf16[64,8,2048]{2,1,0:T(8,128)(2,1)}), bf16[64,8,2048]{2,1,0:T(8,128)(2,1)}, u32[]{:S(2)}, u32[]{:S(2)}) async-start(bf16[64,8,2048]{2,1,0:T(8,128)(2,1)} %fusion.14), calls=%async_computation.3 | async-start | bytes 4194304 | tf_op jit(solution)/shard_map/all_to_all | solution.py:116
  571.2 1047.5 %all-reduce.5.cloned.1.call-start = ((), (), s32[]{:S(2)}) async-start(), calls=%async_computation.6 | async-start | bytes 1048576 | tf_op jit(solution)/shard_map/psum | solution.py:170
  1369.2 2.0 copy-start.6
  1373.2 3.3 copy-start.7
  1374.4 2.1 copy-start.17
  1374.4 2.1 copy-start.19
  1374.4 2.1 copy-start.26
  (9 other events, 6.9 us)
Sparse Core Ops, SparseCore 0:
  547.5 87.0 reduce-scatter.1
Sparse Core Ops, SparseCore 1:
  1373.3 245.4 all-reduce.4
